TPU v7x, 32 devices: a whole 2x2x4 slice. The times are simulated.
32 devices in a mesh: dp: 8 (over y, x, core), tensor: 4 (over z).
Axes of the slice: x: 2, y: 2, z: 4, core: 2. Of those that a mesh axis runs over, the one named last changes fastest.
Arguments:
- resid: bfloat16 [4096, 4096], P('dp', 'tensor'), may hold values from -32 to 32
- hidden: bfloat16 [4096, 14336], P('dp', 'tensor'), may hold values from -6 to 6
- down_weight: bfloat16 [14336, 4096], P('tensor'), may hold values from -1 to 1
- gain: float32 [4096], replicated, may hold values from 0.1 to 1.9
- domain_ids: int32 [8], replicated, may hold values from 0 to 3
Outputs:
- grad_hidden: bfloat16 [4096, 14336], P('dp', 'tensor')
- grad_resid: bfloat16 [4096, 4096], P('dp', 'tensor')
- grad_down: float32 [14336, 4096], P('tensor', 'dp')
- grad_gain: float32 [4096], P('tensor')
All inputs are finite; a program needn't handle non-finite values.
Results may differ from a plain program's by a relative error of at most 0.0034.
Values may be sent and summed in bfloat16 or wider, within the bound.
A program may use at most 192 MiB of HBM per device.

v0:
```python
import jax
import jax.numpy as jnp
from jax import lax
from jax.sharding import PartitionSpec as P

SEQ = 128


score_scale = 20.0
loss_scale = 8192.0
eps_norm = 1e-05
eps_embed = 1e-06
highest = lax.Precision.HIGHEST


def score_gradient(scores, allowed, target):
    weights = jnp.where(allowed, jnp.exp(scores), 0.0)
    soft_weights = weights / jnp.sum(weights, axis=1, keepdims=True)
    return loss_scale * (soft_weights - target.astype(jnp.float32))


def per_device(resid, hidden, down_weight, gain, domain_ids):
    tok_rows = hidden.shape[0]
    model_width = down_weight.shape[1]
    slab_width = model_width // lax.axis_size("tensor")
    tensor_rank = lax.axis_index("tensor")
    shard_rank = lax.axis_index("dp")
    pairs_here = tok_rows // (2 * SEQ)
    offset = tensor_rank * slab_width
    partial_out = jnp.dot(hidden, down_weight, preferred_element_type=jnp.float32)
    own_cols = lax.dynamic_slice_in_dim(partial_out, offset, slab_width, 1) + resid.astype(
        jnp.float32
    )
    partial_out = lax.dynamic_update_slice_in_dim(partial_out, own_cols, offset, 1)
    layer = lax.psum(partial_out, "tensor")
    squares = jnp.sum(layer * layer, axis=1)
    inverse = lax.rsqrt(squares / model_width + eps_norm)
    normed = layer * inverse[:, None] * gain[None, :]
    pooled = jnp.mean(normed.reshape(pairs_here, 2, SEQ, -1), axis=2)
    queries = pooled[:, 0]
    passages = pooled[:, 1]
    total_pairs = pairs_here * lax.axis_size("dp")
    owners = jnp.repeat(domain_ids, pairs_here)
    my_domain = lax.dynamic_slice_in_dim(domain_ids, shard_rank, 1, 0)
    first_own = shard_rank * pairs_here
    own_index = first_own + jnp.arange(pairs_here)
    pair_index = jnp.arange(total_pairs)
    passage_all = lax.all_gather(passages, "dp", axis=0, tiled=True)
    raw_dots = jnp.dot(queries, passage_all.T, precision=highest)
    query_sq = jnp.sum(queries * queries, axis=1)
    passage_sq = jnp.sum(passage_all * passage_all, axis=1)
    query_norm = jnp.sqrt(query_sq + eps_embed)
    passage_norm = jnp.sqrt(passage_sq + eps_embed)
    scores = score_scale * raw_dots / (query_norm[:, None] * passage_norm[None, :])
    allowed = jnp.broadcast_to((owners == my_domain)[None, :], scores.shape)
    target = own_index[:, None] == pair_index[None, :]
    d_score = score_gradient(scores, allowed, target)
    query_unit = queries / query_norm[:, None]
    passage_unit = passage_all / passage_norm[:, None]
    query_coef = jnp.sum(d_score * scores, axis=1)
    d_query = (
        score_scale * jnp.dot(d_score, passage_unit, precision=highest)
        - query_unit * query_coef[:, None]
    ) / query_norm[:, None]
    passage_terms = score_scale * jnp.dot(d_score.T, query_unit, precision=highest)
    passage_coef = jnp.sum(d_score * scores, axis=0)
    passage_sum, coef_sum = (
        lax.psum_scatter(passage_terms, "dp", scatter_dimension=0, tiled=True),
        lax.psum_scatter(passage_coef, "dp", scatter_dimension=0, tiled=True),
    )
    own_unit = lax.dynamic_slice_in_dim(passage_unit, first_own, pairs_here, 0)
    own_norm = lax.dynamic_slice_in_dim(passage_norm, first_own, pairs_here, 0)
    d_passage = (passage_sum - own_unit * coef_sum[:, None]) / own_norm[:, None]
    d_pooled = jnp.stack((d_query, d_passage), axis=1) / SEQ
    d_normed = jnp.broadcast_to(
        d_pooled[:, :, None, :], (pairs_here, 2, SEQ, d_pooled.shape[2])
    ).reshape(tok_rows, -1)
    scaled = d_normed * gain[None, :]
    along = jnp.sum(scaled * layer, axis=1)
    gain_terms = jnp.sum(d_normed * layer * inverse[:, None], axis=0)
    gain_terms = lax.dynamic_slice_in_dim(gain_terms, offset, slab_width, 0)
    grad_gain = lax.psum(gain_terms, "dp")
    d_layer = (
        inverse[:, None] * scaled
        - layer * (inverse * inverse * inverse * along / model_width)[:, None]
    )
    d_low = d_layer.astype(jnp.bfloat16)
    hidden_grad32 = lax.dot_general(
        d_low, down_weight, (((1,), (1,)), ((), ())), preferred_element_type=jnp.float32
    )
    down_part = lax.dot_general(
        hidden, d_low, (((0,), (0,)), ((), ())), preferred_element_type=jnp.float32
    )
    grad_resid = lax.dynamic_slice_in_dim(d_low, offset, slab_width, 1)
    grad_down = lax.psum_scatter(down_part, "dp", scatter_dimension=1, tiled=True)
    return (hidden_grad32.astype(jnp.bfloat16), grad_resid, grad_down, grad_gain)


def solution(mesh):
    return jax.shard_map(
        per_device,
        mesh=mesh,
        in_specs=(P("dp", "tensor"), P("dp", "tensor"), P("tensor", None), P(), P()),
        out_specs=(P("dp", "tensor"), P("dp", "tensor"), P("tensor", "dp"), P("tensor")),
        check_vma=False,
    )
```

profile of v0, /device:TPU:0, one launch (start us, length us, event | category | flops | bytes accessed | tf_op | source)
XLA Modules:
  0.0 780.0 jit_solution(6333060334882277547)
XLA Ops:
  7.2 0.0 all-reduce.5.cloned.1.call-start
  7.2 0.0 copy-start.2
  7.2 23.7 %fusion.23 = f32[512,4096]{1,0:T(8,128)} fusion(bf16[512,3584]{1,0:T(8,128)(2,1)} %param.6, bf16[3584,4096]{1,0:T(8,128)(2,1)} %param.7), kind=kOutput, calls=%fused_computation.51 | convolution fusion | flops 15032385536 | bytes 41418752 | tf_op jit(solution)/shard_map/dot_general | solution.py:30
  30.9 0.0 copy-done.2
  30.9 0.0 copy-start.4
  30.9 0.0 copy-start.5
  30.9 3.4 add_dynamic-update-slice_fusion
  34.3 0.0 copy-start.3
  34.3 0.0 all-reduce.5.cloned.1.call-update
  34.3 0.0 all-reduce.7.cloned.1.call-start
  34.4 0.0 copy-done.4
  34.4 0.6 dynamic_slice.19
  35.0 0.6 broadcast_compare_fusion
  35.6 0.1 broadcast_in_dim.9
  35.7 0.1 eq.34
  35.8 0.0 copy-done.5
  35.8 0.6 dynamic-slice
  37.1 291.0 %all-reduce.5.cloned.1.call-done = f32[512,4096]{1,0:T(8,128)} async-done(((f32[512,4096]{1,0:T(8,128)}), f32[512,4096]{1,0:T(8,128)}) %all-reduce.5.cloned.1.call-update) | async-done | bytes 8388624 | tf_op jit(solution)/shard_map/psum | solution.py:35
  328.0 0.0 copy-start
  328.0 4.2 multiply_reduce_fusion
  332.2 0.0 copy-done.3
  332.2 1.6 copy-done
  333.8 1.3 bitcast_reduce_fusion
  335.1 0.1 copy_multiply_fusion
  335.2 0.1 multiply_reduce_fusion.1
  335.4 9.3 %all-gather = f32[16,1,4096]{2,1,0:T(1,128)S(1)} all-gather(f32[2,1,4096]{2,1,0:T(1,128)S(1)} %copy.14), channel_id=2, replica_groups=mesh['dp'=8,'tensor'=4] {'dp'}, dimensions={0}, use_global_device_ids=true | all-gather | bytes 294912 | tf_op jit(solution)/shard_map/all_gather | solution.py:48
  344.7 0.3 fusion.12
  345.0 0.2 bitcast_divide_fusion
  345.1 0.6 fusion.20
  345.8 0.2 multiply_reduce_fusion.3
  346.0 1.2 convolution_multiply_fusion
  347.1 0.0 all-reduce.7.cloned.1.call-update
  347.1 0.0 reduce-scatter.2.cloned.1.call-start
  347.2 13.4 %all-reduce.1 = f32[16]{0:T(128)S(1)} all-reduce(f32[16]{0:T(128)S(1)} %get-tuple-element.19), channel_id=4, replica_groups=mesh['dp'=8,'tensor'=4] {'dp'}, use_global_device_ids=true, to_apply=%region_9.10.clone | all-reduce | flops 16 | bytes 128
  360.6 0.1 dynamic_slice.21
  360.7 0.1 dynamic-slice.3
  360.8 0.3 fusion.9
  361.0 37.9 %all-reduce.7.cloned.1.call-done = f32[16,4096]{1,0:T(8,128)} async-done(((f32[16,4096]{1,0:T(8,128)}), f32[16,4096]{1,0:T(8,128)}) %all-reduce.7.cloned.1.call-update) | async-done | bytes 262160
  399.0 1.0 fusion.15
  400.0 0.1 copy.15
  400.1 5.0 fusion.6
  405.1 4.3 fusion.3
  409.5 0.0 copy-start.1
  409.5 2.0 copy-done.1
  411.5 24.8 %convolution_bitcast_fusion = f32[3584,4096]{0,1:T(8,128)} fusion(bf16[512,4096]{1,0:T(8,128)(2,1)S(1)} %fusion.3, bf16[512,3584]{1,0:T(8,128)(2,1)} %param.6), kind=kOutput, calls=%fused_computation | convolution fusion | flops 15032385536 | bytes 66584576 | tf_op jit(solution)/shard_map/dot_general | solution.py:91
  436.2 0.0 reduce-scatter.2.cloned.1.call-update
  436.3 12.4 %psum.15 = f32[1024]{0:T(1024)} all-reduce(f32[1024]{0:T(1024)S(1)} %dynamic_slice.23), channel_id=1, replica_groups=mesh['dp'=8,'tensor'=4] {'dp'}, use_global_device_ids=true, to_apply=%region_13.14 | all-reduce | flops 1024 | bytes 8192 | tf_op jit(solution)/shard_map/psum | solution.py:82
  448.7 2.5 constant_dynamic-slice_fusion
  451.2 26.6 %convolution_convert_fusion = bf16[512,3584]{1,0:T(8,128)(2,1)} fusion(bf16[512,4096]{1,0:T(8,128)(2,1)} %copy-done.1, bf16[3584,4096]{1,0:T(8,128)(2,1)} %param.7), kind=kOutput, calls=%fused_computation.13 | convolution fusion | flops 15034220544 | bytes 37224448 | tf_op jit(solution)/shard_map/dot_general | solution.py:88
  477.8 287.3 %reduce-scatter.2.cloned.1.call-done = f32[3584,512]{0,1:T(8,128)} async-done(((f32[3584,4096]{0,1:T(8,128)}), f32[3584,512]{0,1:T(8,128)}) %reduce-scatter.2.cloned.1.call-update) | async-done | bytes 7340048 | tf_op jit(solution)/shard_map/reduce_scatter | solution.py:95
  765.1 8.4 %copy.16 = f32[3584,512]{1,0:T(8,128)} copy(f32[3584,512]{0,1:T(8,128)} %reduce-scatter.2.cloned.1.call-done) | data formatting | bytes 14680064
  (9 shorter events, 0.1 us)
Async XLA Ops:
  7.2 320.8 %all-reduce.5.cloned.1.call-start = ((), (), s32[]{:S(2)}) async-start(), calls=%async_computation.1 | async-start | bytes 16777216 | tf_op jit(solution)/shard_map/psum | solution.py:35
  7.2 23.7 %copy-start.2 = (bf16[512,1024]{1,0:T(8,128)(2,1)S(1)}, bf16[512,1024]{1,0:T(8,128)(2,1)}, u32[]{:S(2)}) copy-start(bf16[512,1024]{1,0:T(8,128)(2,1)} %param.5) | copy-start | bytes 3145732
  30.9 3.5 copy-start.4
  30.9 4.9 copy-start.5
  34.3 297.9 %copy-start.3 = (f32[4096]{0:T(1024)S(1)}, f32[4096]{0:T(1024)}, u32[]{:S(2)}) copy-start(f32[4096]{0:T(1024)} %param.8) | copy-start | bytes 49156
  34.3 364.7 %all-reduce.7.cloned.1.call-start = ((), (), s32[]{:S(2)}) async-start(), calls=%async_computation.3 | async-start | bytes 524288
  328.0 5.8 copy-start
  347.1 418.0 %reduce-scatter.2.cloned.1.call-start = ((), (), s32[]{:S(2)}) async-start(), calls=%async_computation.2 | async-start | bytes 66060288 | tf_op jit(solution)/shard_map/reduce_scatter | solution.py:95
  409.5 2.0 copy-start.1
Sparse Core Ops, SparseCore 0:
  34.4 293.5 all-reduce.4
  347.3 51.6 all-reduce.6
  436.4 328.6 reduce-scatter.1
where the time goes:
time: 780 us
  waiting for transfers between devices  616 us (79%)
  matrix products  77.1 us (10%)
  blocking collectives  35.1 us (4%)
  other arithmetic  20.7 us (3%)
  local copies, waits for them, and re-layouts  16.1 us (2%)
  between operations  14.6 us (2%)
    psum x1, waiting for transfers between devices, per_device(): layer = lax.psum(partial_out, 'tensor')  291 us
    reduce_scatter x1, waiting for transfers between devices, per_device(): lax.psum_scatter(down_part, 'dp', scatter_dimension=1, tiled=True)  287 us
    unnamed x4, waiting for transfers between devices  38 us
    dot_general x1, matrix products, per_device(): lax.dot_general(d_low, down_weight, (((1,), (1,)), ((), ())), preferred_e...  26.6 us
    dot_general x1, matrix products, per_device(): lax.dot_general(hidden, d_low, (((0,), (0,)), ((), ())), preferred_elemen...  24.8 us
    dot_general x1, matrix products, per_device(): jnp.dot(hidden, down_weight, preferred_element_type=jnp.float32)  23.7 us
  transfers between devices with their start and end apart: 3, of which 3 were waited for; matrix products, arithmetic and copies ran while one was open for 4% of the time, Pallas kernels for 0%

commit v1 on v0

v1 whole, which is shorter than its diff:
```python
import jax
import jax.numpy as jnp
from jax import lax
from jax.sharding import PartitionSpec as P

SEQ = 128


score_scale = 20.0
loss_scale = 8192.0
eps_norm = 1e-05
eps_embed = 1e-06
highest = lax.Precision.HIGHEST


def shift_perm(size, step):
    return [(i, (i + step) % size) for i in range(size)]


def flip_perm(size, mask):
    return [(i, i ^ mask) for i in range(size)]


def score_gradient(scores, allowed, target):
    weights = jnp.where(allowed, jnp.exp(scores), 0.0)
    soft_weights = weights / jnp.sum(weights, axis=1, keepdims=True)
    return loss_scale * (soft_weights - target.astype(jnp.float32))


def summed_slab(resid, hidden, down_weight, slab_width, rank, ranks):
    received = []
    for step in list(range(ranks // 2, 0, -1)) + list(range(ranks // 2 + 1, ranks)):
        target = lax.rem(rank + step, ranks)
        block = lax.dynamic_slice_in_dim(down_weight, target * slab_width, slab_width, 1)
        part = jnp.dot(hidden, block, preferred_element_type=jnp.float32)
        row_top = jnp.maximum(jnp.max(jnp.abs(part), axis=1, keepdims=True), 1e-30)
        low = (part / row_top).astype(jnp.float16)
        perm = shift_perm(ranks, step)
        received.append((lax.ppermute(low, "tensor", perm), lax.ppermute(row_top, "tensor", perm)))
    block = lax.dynamic_slice_in_dim(down_weight, rank * slab_width, slab_width, 1)
    layer = jnp.dot(hidden, block, preferred_element_type=jnp.float32) + resid.astype(jnp.float32)
    for low, row_top in received:
        layer = layer + low.astype(jnp.float32) * row_top
    return layer


def gathered_columns(slab, rank, ranks):
    width = slab.shape[1]
    whole = jnp.zeros((slab.shape[0], width * ranks), slab.dtype)
    whole = lax.dynamic_update_slice_in_dim(whole, slab, rank * width, 1)
    for step in range(1, ranks):
        piece = lax.ppermute(slab, "tensor", shift_perm(ranks, step))
        whole = lax.dynamic_update_slice_in_dim(
            whole, piece, lax.rem(rank + ranks - step, ranks) * width, 1
        )
    return whole


def exchanged_tokens(whole, index, count):
    width = whole.shape[1] // count
    blocks = []
    for mask in range(count):
        block = lax.dynamic_slice_in_dim(whole, (index ^ mask) * width, width, 1)
        blocks.append(lax.ppermute(block, "dp", flip_perm(count, mask)) if mask else block)
    return jnp.concatenate(blocks, axis=0)


def gathered_tokens(hidden, count):
    bits = [1 << b for b in range(1, count.bit_length() - 1)]
    rows = hidden.shape[0] // 2
    halves = []
    for part, order in ((hidden[:rows], bits), (hidden[rows:], bits[::-1])):
        pieces = {0: part}
        for bit in order + [1]:
            for mask, piece in list(pieces.items()):
                pieces[mask ^ bit] = lax.ppermute(piece, "dp", flip_perm(count, bit))
        halves.append(pieces)
    return jnp.concatenate([half[mask] for mask in range(count) for half in halves], axis=0)


def pooled_gradient(pooled, domain_ids, pairs_here):
    pairs = pooled.reshape(-1, 2, pooled.shape[1])
    queries = pairs[:, 0]
    passages = pairs[:, 1]
    total_pairs = queries.shape[0]
    owners = jnp.repeat(domain_ids, pairs_here)
    query_norm = jnp.sqrt(jnp.sum(queries * queries, axis=1) + eps_embed)
    passage_norm = jnp.sqrt(jnp.sum(passages * passages, axis=1) + eps_embed)
    query_unit = queries / query_norm[:, None]
    passage_unit = passages / passage_norm[:, None]
    scores = score_scale * jnp.dot(query_unit, passage_unit.T, precision=highest)
    allowed = owners[:, None] == owners[None, :]
    d_score = score_gradient(scores, allowed, jnp.eye(total_pairs))
    weighted = d_score * scores
    d_query = (
        score_scale * jnp.dot(d_score, passage_unit, precision=highest)
        - query_unit * jnp.sum(weighted, axis=1)[:, None]
    ) / query_norm[:, None]
    d_passage = (
        score_scale * jnp.dot(d_score.T, query_unit, precision=highest)
        - passage_unit * jnp.sum(weighted, axis=0)[:, None]
    ) / passage_norm[:, None]
    return jnp.stack((d_query, d_passage), axis=1).reshape(pooled.shape)


def per_device(resid, hidden, down_weight, gain, domain_ids):
    tok_rows = hidden.shape[0]
    model_width = down_weight.shape[1]
    ranks = lax.axis_size("tensor")
    shards = lax.axis_size("dp")
    slab_width = model_width // ranks
    col_width = model_width // shards
    rank = lax.axis_index("tensor")
    shard = lax.axis_index("dp")
    seqs_here = tok_rows // SEQ
    pairs_here = seqs_here // 2

    hidden_all = gathered_tokens(hidden, shards)
    layer = summed_slab(resid, hidden, down_weight, slab_width, rank, ranks)
    layer_low = layer.astype(jnp.bfloat16)
    whole_low = gathered_columns(layer_low, rank, ranks)
    token_cols = exchanged_tokens(whole_low, shard, shards)

    squares = lax.psum(jnp.sum(layer * layer, axis=1), "tensor")
    inverse = lax.rsqrt(squares / model_width + eps_norm)
    raw = jnp.mean((layer * inverse[:, None]).reshape(seqs_here, SEQ, -1), axis=1)
    raw_all = lax.all_gather(raw, ("dp", "tensor"), axis=0, tiled=False)
    raw_all = raw_all.reshape(shards, ranks, seqs_here, slab_width)
    raw_all = jnp.swapaxes(raw_all, 1, 2).reshape(shards * seqs_here, model_width)
    d_pooled = pooled_gradient(raw_all * gain[None, :], domain_ids, pairs_here)
    gain_terms = jnp.sum(d_pooled * raw_all, axis=0)
    grad_gain = lax.dynamic_slice_in_dim(gain_terms, rank * slab_width, slab_width, 0)

    scaled = d_pooled * (gain / SEQ)[None, :]
    scaled_own = lax.dynamic_slice_in_dim(scaled, shard * seqs_here, seqs_here, 0)
    whole_view = whole_low.astype(jnp.float32).reshape(seqs_here, SEQ, model_width)
    along = jnp.sum(scaled_own[:, None, :] * whole_view, axis=2).reshape(tok_rows)
    pull = inverse * inverse * inverse * along / model_width
    own_rows = (
        inverse.reshape(seqs_here, SEQ, 1) * scaled_own[:, None, :]
        - whole_view * pull.reshape(seqs_here, SEQ, 1)
    )
    d_low = own_rows.astype(jnp.bfloat16).reshape(tok_rows, model_width)
    hidden_grad32 = lax.dot_general(
        d_low, down_weight, (((1,), (1,)), ((), ())), preferred_element_type=jnp.float32
    )
    scaled_slab = lax.dynamic_slice_in_dim(scaled_own, rank * slab_width, slab_width, 1)
    grad_resid = (
        inverse.reshape(seqs_here, SEQ, 1) * scaled_slab[:, None, :]
        - layer.reshape(seqs_here, SEQ, slab_width) * pull.reshape(seqs_here, SEQ, 1)
    ).astype(jnp.bfloat16).reshape(tok_rows, slab_width)

    order = shard ^ jnp.arange(shards)
    factors = lax.all_gather(jnp.stack((inverse, pull)), "dp", axis=0, tiled=False)[order]
    inverse_all = factors[:, 0].reshape(shards * seqs_here, SEQ, 1)
    pull_all = factors[:, 1].reshape(shards * seqs_here, SEQ, 1)
    scaled_cols = lax.dynamic_slice_in_dim(scaled, shard * col_width, col_width, 1)
    scaled_cols = scaled_cols.reshape(shards, seqs_here, col_width)[order]
    scaled_cols = scaled_cols.reshape(shards * seqs_here, col_width)
    cols_view = token_cols.astype(jnp.float32).reshape(shards * seqs_here, SEQ, col_width)
    d_cols = (inverse_all * scaled_cols[:, None, :] - cols_view * pull_all).astype(jnp.bfloat16)
    grad_down = lax.dot_general(
        hidden_all,
        d_cols.reshape(shards * tok_rows, col_width),
        (((0,), (0,)), ((), ())),
        preferred_element_type=jnp.float32,
    )
    return (hidden_grad32.astype(jnp.bfloat16), grad_resid, grad_down, grad_gain)


def solution(mesh):
    return jax.shard_map(
        per_device,
        mesh=mesh,
        in_specs=(P("dp", "tensor"), P("dp", "tensor"), P("tensor", None), P(), P()),
        out_specs=(P("dp", "tensor"), P("dp", "tensor"), P("tensor", "dp"), P("tensor")),
        check_vma=False,
    )
```

time: 780 us -> 520 us (0.67); the launches traced: 780 us -> 511 us
  waiting for transfers between devices: 616 us -> 100 us
  blocking collectives: 35.1 us -> 194 us
  local copies, waits for them, and re-layouts: 16.1 us -> 81.9 us
  starting transfers between devices: 0.12 us -> 27.7 us
  between operations: 14.6 us -> 1.43 us
  matrix products: 77.1 us -> 85.6 us
    psum x1 -> x0, waiting for transfers between devices: 291 us -> none  [per_device(): layer = lax.psum(partial_out, 'tensor')]
    reduce_scatter x1 -> x0, waiting for transfers between devices: 287 us -> none  [per_device(): lax.psum_scatter(down_part, 'dp', scatter_dimension=1, tiled=True)]
    all_gather x1 -> x2, blocking collectives: 9.31 us -> 145 us  [the longest x1 89.8 us: per_device(): raw_all = lax.all_gather(raw, ('dp', 'tensor'), axis=0, tiled=False)]
    ppermute x0 -> x30, waiting for transfers between devices: none -> 100 us  [the longest x3 52 us: summed_slab(): lax.ppermute(row_top, 'tensor', perm)]
    unnamed x4 -> x0, waiting for transfers between devices: 38 us -> none
    psum x1, blocking collectives: 12.4 us -> 48.5 us  [per_device(): squares = lax.psum(jnp.sum(layer * layer, axis=1), 'tensor')]
    unnamed x15 -> x31, local copies, waits for them, and re-layouts: 12.6 us -> 47.6 us
    ppermute x0 -> x30, starting transfers between devices: none -> 27.7 us  [the longest x14 9.79 us: gathered_tokens(): pieces[mask ^ bit] = lax.ppermute(piece, 'dp', flip_perm(count, bit))]
  transfers between devices with their start and end apart: 3 -> 30, of which waited for: 3 -> 5; matrix products, arithmetic and copies ran while one was open for 4% -> 30% of each run, Pallas kernels for 0% -> 0%
where the time goes in v1:
time: 520 us; the launch traced here: 511 us
  blocking collectives  194 us (37%)
  waiting for transfers between devices  100 us (19%)
  matrix products  85.6 us (16%)
  local copies, waits for them, and re-layouts  81.9 us (16%)
  starting transfers between devices  27.7 us (5%)
  other arithmetic  20.6 us (4%)
    all_gather x1, blocking collectives, per_device(): raw_all = lax.all_gather(raw, ('dp', 'tensor'), axis=0, tiled=False)  89.8 us
    all_gather x1, blocking collectives, per_device(): lax.all_gather(jnp.stack((inverse, pull)), 'dp', axis=0, tiled=False)[order]  55.5 us
    ppermute x3, waiting for transfers between devices, summed_slab(): lax.ppermute(row_top, 'tensor', perm)  52 us
    psum x1, blocking collectives, per_device(): squares = lax.psum(jnp.sum(layer * layer, axis=1), 'tensor')  48.5 us
    unnamed x31, local copies, waits for them, and re-layouts  47.6 us
    dot_general x3, matrix products, summed_slab(): part = jnp.dot(hidden, block, preferred_element_type=jnp.float32)  28.4 us
    ppermute x7, waiting for transfers between devices, exchanged_tokens(): lax.ppermute(block, 'dp', flip_perm(count, mask))  27.3 us
    dot_general x1, matrix products, per_device(): lax.dot_general(d_low, down_weight, (((1,), (1,)), ((), ())), preferred_e...  23 us
  transfers between devices with their start and end apart: 30, of which 5 were waited for; matrix products, arithmetic and copies ran while one was open for 30% of the time, Pallas kernels for 0%

profile of v1, /device:TPU:0, one launch (start us, length us, event | category | flops | bytes accessed | tf_op | source)
XLA Modules:
  0.0 511.4 jit_solution(1753273479442257240)
XLA Ops:
  0.6 9.5 %abs_reduce_fusion = (f32[512]{0:T(512)S(1)}, f32[1024,512]{1,0:T(8,128)}) fusion(bf16[512,3584]{1,0:T(8,128)(2,1)} %param.6, bf16[3584,4096]{1,0:T(8,128)(2,1)} %param.7, s32[]{:T(128)S(6)} %select_n.68), kind=kOutput, calls=%fused_computation.38 | convolution fusion | flops 3759144448 | bytes 13109252 | tf_op jit(solution)/shard_map/dot_general | solution.py:35
  10.1 5.0 collective-permute-start.5
  15.2 1.9 copy.28
  17.9 9.5 %abs_reduce_fusion.1 = (f32[512]{0:T(512)S(1)}, f32[1024,512]{1,0:T(8,128)}) fusion(bf16[512,3584]{1,0:T(8,128)(2,1)} %param.6, bf16[3584,4096]{1,0:T(8,128)(2,1)} %param.7, s32[]{:T(128)S(6)} %select_n.67), kind=kOutput, calls=%fused_computation.40 | convolution fusion | flops 3759144448 | bytes 13109252 | tf_op jit(solution)/shard_map/dot_general | solution.py:35
  27.4 1.6 collective-permute-start.3
  29.0 1.9 copy.27
  30.9 1.3 fusion.25
  32.4 9.5 %abs_reduce_fusion.2 = (f32[512]{0:T(512)S(1)}, f32[1024,512]{1,0:T(8,128)}) fusion(bf16[512,3584]{1,0:T(8,128)(2,1)} %param.6, bf16[3584,4096]{1,0:T(8,128)(2,1)} %param.7, s32[]{:T(128)S(6)} %select_n.66), kind=kOutput, calls=%fused_computation.42 | convolution fusion | flops 3759144448 | bytes 13109252 | tf_op jit(solution)/shard_map/dot_general | solution.py:35
  41.9 1.9 copy.26
  43.8 1.3 fusion.24
  45.1 2.8 collective-permute-start
  47.9 4.1 constant_dynamic-update-slice_fusion.14
  52.0 4.1 fusion.48
  56.6 51.9 %collective-permute-done.1 = f32[512,1]{0,1:T(1,128)S(1)} collective-permute-done((f32[512,1]{0,1:T(1,128)S(1)}, f32[512,1]{0,1:T(1,128)S(1)}, u32[]{:S(2)}, u32[]{:S(2)}) %collective-permute-start.1) | collective-permute-done | bytes 2080 | tf_op jit(solution)/shard_map/ppermute | solution.py:39
  108.5 1.5 collective-permute-start.11
  111.1 2.5 broadcast_in_dim.9
  113.6 9.8 %constant_dynamic-update-slice_fusion.25 = (bf16[512,4096]{1,0:T(8,128)(2,1)}, bf16[512,1024]{1,0:T(8,128)(2,1)}, f32[512,1024]{1,0:T(8,128)S(1)}) fusion(bf16[512,4096]{1,0:T(8,128)(2,1)} %broadcast_in_dim.9, s32[]{:T(128)S(6)} %select_n.65, f32[512]{0:T(512)S(1)} %bitcast.107, f16[512,1024]{1,0:T(8,128)(2,1)} %collective-permute-done.4, ...), kind=kOutput, calls=%fused_computation.108 | convolution fusion | flops 3764387840 | bytes 19405824 | tf_op jit(solution)/shard_map/dot_general | solution.py:41
  124.0 3.3 collective-permute-start.7
  127.5 48.5 %psum.7 = f32[512]{0:T(512)S(1)} all-reduce(f32[512]{0:T(512)S(1)} %multiply_reduce_fusion), channel_id=1, replica_groups=mesh['dp'=8,'tensor'=4] {'tensor'}, use_global_device_ids=true, to_apply=%region_4.0 | all-reduce | flops 512 | bytes 4096 | tf_op jit(solution)/shard_map/psum | solution.py:124
  176.2 89.8 %all-gather.2 = f32[32,4,1024]{2,1,0:T(4,128)S(1)} all-gather(f32[1,4,1024]{2,1,0:T(4,128)S(1)} %multiply_bitcast_fusion), channel_id=2, replica_groups=mesh['dp'=8,'tensor'=4] {'dp','tensor'}, dimensions={0}, use_global_device_ids=true | all-gather | bytes 540672 | tf_op jit(solution)/shard_map/all_gather | solution.py:127
  267.2 1.6 reshape.157
  271.5 1.2 reshape.158
  274.6 1.3 stack.26
  276.6 1.7 fusion.27
  279.9 1.6 collective-permute-start.16
  281.5 2.9 constant_dynamic-update-slice_fusion.13
  284.4 2.3 constant_dynamic-update-slice_fusion.24
  286.6 2.3 constant_dynamic-update-slice_fusion.23
  288.9 5.5 %collective-permute-done.8 = bf16[512,1024]{1,0:T(8,128)(2,1)} collective-permute-done((bf16[512,1024]{1,0:T(8,128)(2,1)}, bf16[512,1024]{1,0:T(8,128)(2,1)}, u32[]{:S(2)}, u32[]{:S(2)}) %collective-permute-start.8) | collective-permute-done | bytes 1048608 | tf_op jit(solution)/shard_map/ppermute | solution.py:52
  294.4 2.3 constant_dynamic-update-slice_fusion.22
  296.6 3.3 constant_dynamic-slice_fusion
  300.0 2.9 constant_dynamic-update-slice_fusion.12
  302.9 2.9 constant_dynamic-update-slice_fusion.11
  305.8 1.8 collective-permute-start.25
  307.6 15.5 %collective-permute-done.12 = bf16[256,3584]{1,0:T(8,128)(2,1)} collective-permute-done((bf16[256,3584]{1,0:T(8,128)(2,1)}, bf16[256,3584]{1,0:T(8,128)(2,1)}, u32[]{:S(2)}, u32[]{:S(2)}) %collective-permute-start.12) | collective-permute-done | bytes 1835040 | tf_op jit(solution)/shard_map/ppermute | solution.py:76
  323.1 1.6 collective-permute-start.26
  324.8 9.5 %collective-permute-done.24 = bf16[512,512]{1,0:T(8,128)(2,1)S(1)} collective-permute-done((bf16[512,512]{1,0:T(8,128)(2,1)S(1)}, bf16[512,512]{1,0:T(8,128)(2,1)S(1)}, u32[]{:S(2)}, u32[]{:S(2)}) %collective-permute-start.24) | collective-permute-done | bytes 524320 | tf_op jit(solution)/shard_map/ppermute | solution.py:64
  334.3 2.9 constant_dynamic-update-slice_fusion.10
  337.1 3.1 fusion.2
  340.2 6.3 %fusion.1 = bf16[512,4096]{1,0:T(8,128)(2,1)} fusion(bf16[512,4096]{1,0:T(8,128)(2,1)} %constant_dynamic-update-slice_fusion.22, f32[512]{0:T(512)S(1)} %fusion.46, f32[4,4096]{1,0:T(4,128)S(1)} %constant_dynamic-slice_fusion.8, f32[512]{0:T(512)S(1)} %add_rsqrt_fusion), kind=kLoop, calls=%fused_computation.6 | loop fusion | flops 10485760 | bytes 8458240 | tf_op jit(solution)/shard_map/convert_element_type | solution.py:143
  346.5 1.6 collective-permute-start.15
  348.1 17.8 %collective-permute-done.27 = bf16[512,512]{1,0:T(8,128)(2,1)} collective-permute-done((bf16[512,512]{1,0:T(8,128)(2,1)S(1)}, bf16[512,512]{1,0:T(8,128)(2,1)}, u32[]{:S(2)}, u32[]{:S(2)}) %collective-permute-start.27) | collective-permute-done | bytes 524320 | tf_op jit(solution)/shard_map/ppermute | solution.py:64
  365.9 1.9 collective-permute-start.14
  368.3 1.5 collective-permute-start.20
  369.8 23.0 %convolution_convert_fusion = bf16[512,3584]{1,0:T(8,128)(2,1)} fusion(bf16[512,4096]{1,0:T(8,128)(2,1)} %fusion.1, bf16[3584,4096]{1,0:T(8,128)(2,1)} %param.7), kind=kOutput, calls=%fused_computation.19 | convolution fusion | flops 15034220544 | bytes 37224448 | tf_op jit(solution)/shard_map/dot_general | solution.py:144
  392.8 1.3 fusion.20
  394.1 55.5 %all-gather.3 = f32[8,2,512]{2,1,0:T(2,128)S(1)} all-gather(f32[1,2,512]{2,1,0:T(2,128)S(1)} %maximum_bitcast_fusion), channel_id=3, replica_groups=mesh['dp'=8,'tensor'=4] {'dp'}, dimensions={0}, use_global_device_ids=true | all-gather | bytes 36864 | tf_op jit(solution)/shard_map/all_gather | solution.py:154
  451.9 1.9 constant_dynamic-update-slice_fusion.19
  453.8 1.9 constant_dynamic-update-slice_fusion.18
  455.6 1.9 constant_dynamic-update-slice_fusion.17
  457.5 1.9 constant_dynamic-update-slice_fusion.16
  459.4 1.9 constant_dynamic-update-slice_fusion.15
  461.2 3.0 fusion.4
  465.4 2.9 constant_dynamic-update-slice_fusion.9
  468.2 2.9 constant_dynamic-update-slice_fusion.8
  471.1 2.9 constant_dynamic-update-slice_fusion.7
  473.9 2.9 constant_dynamic-update-slice_fusion.6
  476.8 1.3 constant_dynamic-update-slice_fusion.5
  478.1 1.4 constant_dynamic-update-slice_fusion.4
  479.5 2.9 constant_dynamic-update-slice_fusion.3
  482.4 2.9 constant_dynamic-update-slice_fusion.2
  485.4 1.4 constant_dynamic-update-slice_fusion.1
  486.8 1.4 constant_dynamic-update-slice_fusion
  488.1 22.8 %fusion.50 = f32[3584,512]{1,0:T(8,128)} fusion(bf16[4096,3584]{1,0:T(8,128)(2,1)} %constant_dynamic-update-slice_fusion, bf16[4096,512]{1,0:T(8,128)(2,1)S(1)} %fusion.4), kind=kOutput, calls=%fused_computation.131 | convolution fusion | flops 15032385536 | bytes 40894464 | tf_op jit(solution)/shard_map/dot_general | solution.py:162
  (92 shorter events, 15.5 us)
Async XLA Ops:
  10.1 46.0 %collective-permute-start.5 = (f32[512,1]{0,1:T(1,128)S(1)}, f32[512,1]{0,1:T(1,128)S(1)}, u32[]{:S(2)}, u32[]{:S(2)}) collective-permute-start(f32[512,1]{0,1:T(1,128)S(1)} %bitcast.106), channel_id=1, source_target_pairs={{0,3},{1,0},{2,1},{3,2},{4,7},{5,4},{6,5},{7,6},{8,11},{9,8},{10,9... | collective-permute-start | bytes 6152 | tf_op jit(solution)/shard_map/ppermute | solution.py:39
  17.4 92.6 %collective-permute-start.4 = (f16[512,1024]{1,0:T(8,128)(2,1)S(1)}, f16[512,1024]{1,0:T(8,128)(2,1)}, u32[]{:S(2)}, u32[]{:S(2)}) collective-permute-start(f16[512,1024]{1,0:T(8,128)(2,1)S(1)} %fusion.26), channel_id=1, source_target_pairs={{0,3},{1,0},{2,1},{3,2},{4,7},{5,4},{6,5},{7,6},{8,11},{9,8},{10,9... | collective-permute-start | bytes 3145736 | tf_op jit(solution)/shard_map/ppermute | solution.py:39
  27.4 29.1 %collective-permute-start.3 = (f32[512,1]{0,1:T(1,128)S(1)}, f32[512,1]{0,1:T(1,128)S(1)}, u32[]{:S(2)}, u32[]{:S(2)}) collective-permute-start(f32[512,1]{0,1:T(1,128)S(1)} %bitcast.104), channel_id=1, source_target_pairs={{0,1},{1,2},{2,3},{3,0},{4,5},{5,6},{6,7},{7,4},{8,9},{9,10},{10,1... | collective-permute-start | bytes 6152 | tf_op jit(solution)/shard_map/ppermute | solution.py:39
  32.2 77.8 %collective-permute-start.2 = (f16[512,1024]{1,0:T(8,128)(2,1)}, f16[512,1024]{1,0:T(8,128)(2,1)}, u32[]{:S(2)}, u32[]{:S(2)}) collective-permute-start(f16[512,1024]{1,0:T(8,128)(2,1)} %fusion.25), channel_id=1, source_target_pairs={{0,1},{1,2},{2,3},{3,0},{4,5},{5,6},{6,7},{7,4},{8,9},{9,10},{10,1... | collective-permute-start | bytes 3145736 | tf_op jit(solution)/shard_map/ppermute | solution.py:39
  45.1 6.8 %copy-start.2 = (f32[4096]{0:T(1024)S(1)}, f32[4096]{0:T(1024)}, u32[]{:S(2)}) copy-start(f32[4096]{0:T(1024)} %param.8) | copy-start | bytes 49156
  45.1 64.9 %collective-permute-start = (f16[512,1024]{1,0:T(8,128)(2,1)}, f16[512,1024]{1,0:T(8,128)(2,1)S(1)}, u32[]{:S(2)}, u32[]{:S(2)}) collective-permute-start(f16[512,1024]{1,0:T(8,128)(2,1)} %fusion.24), channel_id=1, source_target_pairs={{0,2},{1,3},{2,0},{3,1},{4,6},{5,7},{6,4},{7,5},{8,10},{9,11},{10,... | collective-permute-start | bytes 3145736 | tf_op jit(solution)/shard_map/ppermute | solution.py:39
  52.0 4.4 copy-start.3
  56.1 52.4 %collective-permute-start.1 = (f32[512,1]{0,1:T(1,128)S(1)}, f32[512,1]{0,1:T(1,128)S(1)}, u32[]{:S(2)}, u32[]{:S(2)}) collective-permute-start(f32[512,1]{0,1:T(1,128)S(1)} %bitcast.105), channel_id=1, source_target_pairs={{0,2},{1,3},{2,0},{3,1},{4,6},{5,7},{6,4},{7,5},{8,10},{9,11},{10,... | collective-permute-start | bytes 6152 | tf_op jit(solution)/shard_map/ppermute | solution.py:39
  56.5 57.1 %copy-start = (bf16[512,3584]{1,0:T(8,128)(2,1)S(1)}, bf16[512,3584]{1,0:T(8,128)(2,1)}, u32[]{:S(2)}) copy-start(bf16[512,3584]{1,0:T(8,128)(2,1)} %param.6) | copy-start | bytes 11010052
  56.5 217.3 %collective-permute-start.9 = (bf16[256,3584]{1,0:T(8,128)(2,1)}, bf16[256,3584]{1,0:T(8,128)(2,1)}, u32[]{:S(2)}, u32[]{:S(2)}) collective-permute-start(bf16[256,3584]{1,0:T(8,128)(2,1)} %get-tuple-element.19), channel_id=1, source_target_pairs={{0,4},{4,0},{8,12},{12,8},{16,20},{20,16},{24,28},{28,24},{1,5},{5... | collective-permute-start | bytes 5505032 | tf_op jit(solution)/shard_map/ppermute | solution.py:76
  108.5 194.3 %collective-permute-start.11 = (bf16[256,3584]{1,0:T(8,128)(2,1)}, bf16[256,3584]{1,0:T(8,128)(2,1)}, u32[]{:S(2)}, u32[]{:S(2)}) collective-permute-start(bf16[256,3584]{1,0:T(8,128)(2,1)} %get-tuple-element.19), channel_id=1, source_target_pairs={{0,8},{4,12},{8,0},{12,4},{16,24},{20,28},{24,16},{28,20},{1,9},{5... | collective-permute-start | bytes 5505032 | tf_op jit(solution)/shard_map/ppermute | solution.py:76
  110.1 189.8 %collective-permute-start.10 = (bf16[256,3584]{1,0:T(8,128)(2,1)}, bf16[256,3584]{1,0:T(8,128)(2,1)}, u32[]{:S(2)}, u32[]{:S(2)}) collective-permute-start(bf16[256,3584]{1,0:T(8,128)(2,1)} %get-tuple-element.18), channel_id=1, source_target_pairs={{0,4},{4,0},{8,12},{12,8},{16,20},{20,16},{24,28},{28,24},{1,5},{5... | collective-permute-start | bytes 5505032 | tf_op jit(solution)/shard_map/ppermute | solution.py:76
  110.1 1.0 copy-start.4
  123.4 156.4 %collective-permute-start.6 = (bf16[512,1024]{1,0:T(8,128)(2,1)}, bf16[512,1024]{1,0:T(8,128)(2,1)}, u32[]{:S(2)}, u32[]{:S(2)}) collective-permute-start(bf16[512,1024]{1,0:T(8,128)(2,1)} %get-tuple-element.9), channel_id=1, source_target_pairs={{0,1},{1,2},{2,3},{3,0},{4,5},{5,6},{6,7},{7,4},{8,9},{9,10},{10,1... | collective-permute-start | bytes 3145736 | tf_op jit(solution)/shard_map/ppermute | solution.py:52
  124.0 155.9 %collective-permute-start.7 = (bf16[512,1024]{1,0:T(8,128)(2,1)}, bf16[512,1024]{1,0:T(8,128)(2,1)}, u32[]{:S(2)}, u32[]{:S(2)}) collective-permute-start(bf16[512,1024]{1,0:T(8,128)(2,1)} %get-tuple-element.9), channel_id=1, source_target_pairs={{0,2},{1,3},{2,0},{3,1},{4,6},{5,7},{6,4},{7,5},{8,10},{9,11},{10,... | collective-permute-start | bytes 3145736 | tf_op jit(solution)/shard_map/ppermute | solution.py:52
  273.8 0.8 copy-start.1
  273.8 20.6 %collective-permute-start.8 = (bf16[512,1024]{1,0:T(8,128)(2,1)}, bf16[512,1024]{1,0:T(8,128)(2,1)}, u32[]{:S(2)}, u32[]{:S(2)}) collective-permute-start(bf16[512,1024]{1,0:T(8,128)(2,1)} %get-tuple-element.9), channel_id=1, source_target_pairs={{0,3},{1,0},{2,1},{3,2},{4,7},{5,4},{6,5},{7,6},{8,11},{9,8},{10,9... | collective-permute-start | bytes 3145736 | tf_op jit(solution)/shard_map/ppermute | solution.py:52
  279.8 43.3 %collective-permute-start.12 = (bf16[256,3584]{1,0:T(8,128)(2,1)}, bf16[256,3584]{1,0:T(8,128)(2,1)}, u32[]{:S(2)}, u32[]{:S(2)}) collective-permute-start(bf16[256,3584]{1,0:T(8,128)(2,1)} %get-tuple-element.18), channel_id=1, source_target_pairs={{0,8},{4,12},{8,0},{12,4},{16,24},{20,28},{24,16},{28,20},{1,9},{5... | collective-permute-start | bytes 5505032 | tf_op jit(solution)/shard_map/ppermute | solution.py:76
  279.9 44.8 %collective-permute-start.16 = (bf16[256,3584]{1,0:T(8,128)(2,1)}, bf16[256,3584]{1,0:T(8,128)(2,1)}, u32[]{:S(2)}, u32[]{:S(2)}) collective-permute-start(bf16[256,3584]{1,0:T(8,128)(2,1)} %get-tuple-element.18), channel_id=1, source_target_pairs={{0,16},{4,20},{8,24},{12,28},{16,0},{20,4},{24,8},{28,12},{1,17},{... | collective-permute-start | bytes 5505032 | tf_op jit(solution)/shard_map/ppermute | solution.py:76
  299.9 24.8 %collective-permute-start.23 = (bf16[512,512]{1,0:T(8,128)(2,1)S(1)}, bf16[512,512]{1,0:T(8,128)(2,1)S(1)}, u32[]{:S(2)}, u32[]{:S(2)}) collective-permute-start(bf16[512,512]{1,0:T(8,128)(2,1)S(1)} %get-tuple-element.16), channel_id=1, source_target_pairs={{0,4},{4,0},{8,12},{12,8},{16,20},{20,16},{24,28},{28,24},{1,5},{5... | collective-permute-start | bytes 1572872 | tf_op jit(solution)/shard_map/ppermute | solution.py:64
  299.9 34.3 %collective-permute-start.24 = (bf16[512,512]{1,0:T(8,128)(2,1)S(1)}, bf16[512,512]{1,0:T(8,128)(2,1)S(1)}, u32[]{:S(2)}, u32[]{:S(2)}) collective-permute-start(bf16[512,512]{1,0:T(8,128)(2,1)S(1)} %get-tuple-element.15), channel_id=1, source_target_pairs={{0,8},{4,12},{8,0},{12,4},{16,24},{20,28},{24,16},{28,20},{1,9},{5... | collective-permute-start | bytes 1572872 | tf_op jit(solution)/shard_map/ppermute | solution.py:64
  305.8 40.7 %collective-permute-start.25 = (bf16[512,512]{1,0:T(8,128)(2,1)S(1)}, bf16[512,512]{1,0:T(8,128)(2,1)}, u32[]{:S(2)}, u32[]{:S(2)}) collective-permute-start(bf16[512,512]{1,0:T(8,128)(2,1)S(1)} %get-tuple-element.14), channel_id=1, source_target_pairs={{0,12},{4,8},{8,4},{12,0},{16,28},{20,24},{24,20},{28,16},{1,13},{... | collective-permute-start | bytes 1572872 | tf_op jit(solution)/shard_map/ppermute | solution.py:64
  323.1 25.0 %collective-permute-start.26 = (bf16[512,512]{1,0:T(8,128)(2,1)S(1)}, bf16[512,512]{1,0:T(8,128)(2,1)}, u32[]{:S(2)}, u32[]{:S(2)}) collective-permute-start(bf16[512,512]{1,0:T(8,128)(2,1)S(1)} %get-tuple-element.13), channel_id=1, source_target_pairs={{0,16},{4,20},{8,24},{12,28},{16,0},{20,4},{24,8},{28,12},{1,17},{... | collective-permute-start | bytes 1572872 | tf_op jit(solution)/shard_map/ppermute | solution.py:64
  324.7 41.2 %collective-permute-start.27 = (bf16[512,512]{1,0:T(8,128)(2,1)S(1)}, bf16[512,512]{1,0:T(8,128)(2,1)}, u32[]{:S(2)}, u32[]{:S(2)}) collective-permute-start(bf16[512,512]{1,0:T(8,128)(2,1)S(1)} %get-tuple-element.12), channel_id=1, source_target_pairs={{0,20},{4,16},{8,28},{12,24},{16,4},{20,0},{24,12},{28,8},{1,21},{... | collective-permute-start | bytes 1572872 | tf_op jit(solution)/shard_map/ppermute | solution.py:64
  324.7 43.1 %collective-permute-start.28 = (bf16[512,512]{1,0:T(8,128)(2,1)S(1)}, bf16[512,512]{1,0:T(8,128)(2,1)}, u32[]{:S(2)}, u32[]{:S(2)}) collective-permute-start(bf16[512,512]{1,0:T(8,128)(2,1)S(1)} %get-tuple-element.11), channel_id=1, source_target_pairs={{0,24},{4,28},{8,16},{12,20},{16,8},{20,12},{24,0},{28,4},{1,25},{... | collective-permute-start | bytes 1572872 | tf_op jit(solution)/shard_map/ppermute | solution.py:64
  334.3 34.1 %collective-permute-start.29 = (bf16[512,512]{1,0:T(8,128)(2,1)S(1)}, bf16[512,512]{1,0:T(8,128)(2,1)}, u32[]{:S(2)}, u32[]{:S(2)}) collective-permute-start(bf16[512,512]{1,0:T(8,128)(2,1)S(1)} %get-tuple-element.10), channel_id=1, source_target_pairs={{0,28},{4,24},{8,20},{12,16},{16,12},{20,8},{24,4},{28,0},{1,29},{... | collective-permute-start | bytes 1572872 | tf_op jit(solution)/shard_map/ppermute | solution.py:64
  346.5 117.7 %collective-permute-start.15 = (bf16[256,3584]{1,0:T(8,128)(2,1)}, bf16[256,3584]{1,0:T(8,128)(2,1)}, u32[]{:S(2)}, u32[]{:S(2)}) collective-permute-start(bf16[256,3584]{1,0:T(8,128)(2,1)} %get-tuple-element.19), channel_id=1, source_target_pairs={{0,16},{4,20},{8,24},{12,28},{16,0},{20,4},{24,8},{28,12},{1,17},{... | collective-permute-start | bytes 5505032 | tf_op jit(solution)/shard_map/ppermute | solution.py:76
  348.1 116.6 %collective-permute-start.13 = (bf16[256,3584]{1,0:T(8,128)(2,1)}, bf16[256,3584]{1,0:T(8,128)(2,1)}, u32[]{:S(2)}, u32[]{:S(2)}) collective-permute-start(bf16[256,3584]{1,0:T(8,128)(2,1)} %collective-permute-done.11), channel_id=1, source_target_pairs={{0,4},{4,0},{8,12},{12,8},{16,20},{20,16},{24,28},{28,24},{1,5},{5... | collective-permute-start | bytes 5505032 | tf_op jit(solution)/shard_map/ppermute | solution.py:76
  365.9 102.3 %collective-permute-start.14 = (bf16[256,3584]{1,0:T(8,128)(2,1)}, bf16[256,3584]{1,0:T(8,128)(2,1)}, u32[]{:S(2)}, u32[]{:S(2)}) collective-permute-start(bf16[256,3584]{1,0:T(8,128)(2,1)} %collective-permute-done.12), channel_id=1, source_target_pairs={{0,4},{4,0},{8,12},{12,8},{16,20},{20,16},{24,28},{28,24},{1,5},{5... | collective-permute-start | bytes 5505032 | tf_op jit(solution)/shard_map/ppermute | solution.py:76
  367.8 97.0 %collective-permute-start.19 = (bf16[256,3584]{1,0:T(8,128)(2,1)}, bf16[256,3584]{1,0:T(8,128)(2,1)}, u32[]{:S(2)}, u32[]{:S(2)}) collective-permute-start(bf16[256,3584]{1,0:T(8,128)(2,1)} %collective-permute-done.11), channel_id=1, source_target_pairs={{0,16},{4,20},{8,24},{12,28},{16,0},{20,4},{24,8},{28,12},{1,17},{... | collective-permute-start | bytes 5505032 | tf_op jit(solution)/shard_map/ppermute | solution.py:76
  368.3 96.9 %collective-permute-start.20 = (bf16[256,3584]{1,0:T(8,128)(2,1)}, bf16[256,3584]{1,0:T(8,128)(2,1)}, u32[]{:S(2)}, u32[]{:S(2)}) collective-permute-start(bf16[256,3584]{1,0:T(8,128)(2,1)} %collective-permute-done.16), channel_id=1, source_target_pairs={{0,8},{4,12},{8,0},{12,4},{16,24},{20,28},{24,16},{28,20},{1,9},{5... | collective-permute-start | bytes 5505032 | tf_op jit(solution)/shard_map/ppermute | solution.py:76
  464.3 13.9 %collective-permute-start.18 = (bf16[256,3584]{1,0:T(8,128)(2,1)}, bf16[256,3584]{1,0:T(8,128)(2,1)S(1)}, u32[]{:S(2)}, u32[]{:S(2)}) collective-permute-start(bf16[256,3584]{1,0:T(8,128)(2,1)} %collective-permute-done.16), channel_id=1, source_target_pairs={{0,4},{4,0},{8,12},{12,8},{16,20},{20,16},{24,28},{28,24},{1,5},{5... | collective-permute-start | bytes 5505032 | tf_op jit(solution)/shard_map/ppermute | solution.py:76
  464.7 12.1 %collective-permute-start.17 = (bf16[256,3584]{1,0:T(8,128)(2,1)}, bf16[256,3584]{1,0:T(8,128)(2,1)S(1)}, u32[]{:S(2)}, u32[]{:S(2)}) collective-permute-start(bf16[256,3584]{1,0:T(8,128)(2,1)} %collective-permute-done.15), channel_id=1, source_target_pairs={{0,4},{4,0},{8,12},{12,8},{16,20},{20,16},{24,28},{28,24},{1,5},{5... | collective-permute-start | bytes 5505032 | tf_op jit(solution)/shard_map/ppermute | solution.py:76
  464.8 20.5 %collective-permute-start.21 = (bf16[256,3584]{1,0:T(8,128)(2,1)}, bf16[256,3584]{1,0:T(8,128)(2,1)S(1)}, u32[]{:S(2)}, u32[]{:S(2)}) collective-permute-start(bf16[256,3584]{1,0:T(8,128)(2,1)} %collective-permute-done.19), channel_id=1, source_target_pairs={{0,4},{4,0},{8,12},{12,8},{16,20},{20,16},{24,28},{28,24},{1,5},{5... | collective-permute-start | bytes 5505032 | tf_op jit(solution)/shard_map/ppermute | solution.py:76
  465.2 21.6 %collective-permute-start.22 = (bf16[256,3584]{1,0:T(8,128)(2,1)}, bf16[256,3584]{1,0:T(8,128)(2,1)S(1)}, u32[]{:S(2)}, u32[]{:S(2)}) collective-permute-start(bf16[256,3584]{1,0:T(8,128)(2,1)} %collective-permute-done.20), channel_id=1, source_target_pairs={{0,4},{4,0},{8,12},{12,8},{16,20},{20,16},{24,28},{28,24},{1,5},{5... | collective-permute-start | bytes 5505032 | tf_op jit(solution)/shard_map/ppermute | solution.py:76

commit v2 on v1

--- a/solution.py
+++ b/solution.py
@@ -57,25 +57,16 @@
 
 
 def exchanged_tokens(whole, index, count):
+    rows = whole.shape[0]
     width = whole.shape[1] // count
-    blocks = []
+    tokens = jnp.zeros((count, rows, width), whole.dtype)
     for mask in range(count):
-        block = lax.dynamic_slice_in_dim(whole, (index ^ mask) * width, width, 1)
-        blocks.append(lax.ppermute(block, "dp", flip_perm(count, mask)) if mask else block)
-    return jnp.concatenate(blocks, axis=0)
-
-
-def gathered_tokens(hidden, count):
-    bits = [1 << b for b in range(1, count.bit_length() - 1)]
-    rows = hidden.shape[0] // 2
-    halves = []
-    for part, order in ((hidden[:rows], bits), (hidden[rows:], bits[::-1])):
-        pieces = {0: part}
-        for bit in order + [1]:
-            for mask, piece in list(pieces.items()):
-                pieces[mask ^ bit] = lax.ppermute(piece, "dp", flip_perm(count, bit))
-        halves.append(pieces)
-    return jnp.concatenate([half[mask] for mask in range(count) for half in halves], axis=0)
+        other = index ^ mask
+        block = lax.dynamic_slice_in_dim(whole, other * width, width, 1)
+        if mask:
+            block = lax.ppermute(block, "dp", flip_perm(count, mask))
+        tokens = lax.dynamic_update_slice_in_dim(tokens, block[None], other, 0)
+    return tokens
 
 
 def pooled_gradient(pooled, domain_ids, pairs_here):
@@ -115,13 +106,12 @@
     seqs_here = tok_rows // SEQ
     pairs_here = seqs_here // 2
 
-    hidden_all = gathered_tokens(hidden, shards)
+    hidden_all = lax.all_gather(hidden, "dp", axis=0, tiled=True)
     layer = summed_slab(resid, hidden, down_weight, slab_width, rank, ranks)
-    layer_low = layer.astype(jnp.bfloat16)
+    squares = lax.psum(jnp.sum(layer * layer, axis=1), "tensor")
+    squares, layer_low = lax.optimization_barrier((squares, layer.astype(jnp.bfloat16)))
     whole_low = gathered_columns(layer_low, rank, ranks)
     token_cols = exchanged_tokens(whole_low, shard, shards)
-
-    squares = lax.psum(jnp.sum(layer * layer, axis=1), "tensor")
     inverse = lax.rsqrt(squares / model_width + eps_norm)
     raw = jnp.mean((layer * inverse[:, None]).reshape(seqs_here, SEQ, -1), axis=1)
     raw_all = lax.all_gather(raw, ("dp", "tensor"), axis=0, tiled=False)
@@ -150,13 +140,10 @@
         - layer.reshape(seqs_here, SEQ, slab_width) * pull.reshape(seqs_here, SEQ, 1)
     ).astype(jnp.bfloat16).reshape(tok_rows, slab_width)
 
-    order = shard ^ jnp.arange(shards)
-    factors = lax.all_gather(jnp.stack((inverse, pull)), "dp", axis=0, tiled=False)[order]
+    factors = lax.all_gather(jnp.stack((inverse, pull)), "dp", axis=0, tiled=False)
     inverse_all = factors[:, 0].reshape(shards * seqs_here, SEQ, 1)
     pull_all = factors[:, 1].reshape(shards * seqs_here, SEQ, 1)
     scaled_cols = lax.dynamic_slice_in_dim(scaled, shard * col_width, col_width, 1)
-    scaled_cols = scaled_cols.reshape(shards, seqs_here, col_width)[order]
-    scaled_cols = scaled_cols.reshape(shards * seqs_here, col_width)
     cols_view = token_cols.astype(jnp.float32).reshape(shards * seqs_here, SEQ, col_width)
     d_cols = (inverse_all * scaled_cols[:, None, :] - cols_view * pull_all).astype(jnp.bfloat16)
     grad_down = lax.dot_general(

time: 520 us -> 455 us (0.88)
  local copies, waits for them, and re-layouts: 81.9 us -> 34.4 us
  waiting for transfers between devices: 100 us -> 60.5 us
  starting transfers between devices: 27.7 us -> 43.2 us
  between operations: 1.43 us -> 14.9 us
  blocking collectives: 194 us -> 188 us
    all_gather x1, blocking collectives: 89.8 us -> 149 us  [per_device(): raw_all = lax.all_gather(raw, ('dp', 'tensor'), axis=0, tiled=False)]
    unnamed x31 -> x10, local copies, waits for them, and re-layouts: 47.6 us -> 9.34 us
    psum x1, blocking collectives: 48.5 us -> 12.3 us  [per_device(): squares = lax.psum(jnp.sum(layer * layer, axis=1), 'tensor')]
    all_gather x1, blocking collectives: 55.5 us -> 26.7 us  [per_device(): lax.all_gather(jnp.stack((inverse, pull)), 'dp', axis=0, tiled=False)]
    ppermute x21 -> x7, waiting for transfers between devices: 42.9 us -> 21.8 us  [exchanged_tokens(): block = lax.ppermute(block, 'dp', flip_perm(count, mask))]
    ppermute x3, starting transfers between devices: 6.84 us -> 25.4 us  [summed_slab(): lax.ppermute(row_top, 'tensor', perm)]
    ppermute x3, waiting for transfers between devices: 52 us -> 38 us  [summed_slab(): lax.ppermute(row_top, 'tensor', perm)]
    ppermute x21 -> x7, starting transfers between devices: 13.3 us -> 6.42 us  [exchanged_tokens(): block = lax.ppermute(block, 'dp', flip_perm(count, mask))]
  transfers between devices with their start and end apart: 30 -> 17, of which waited for: 5 -> 4; matrix products, arithmetic and copies ran while one was open for 30% -> 24% of each run, Pallas kernels for 0% -> 0%
where the time goes in v2:
time: 455 us; the launch traced here: 447 us
  blocking collectives  188 us (41%)
  matrix products  89 us (20%)
  waiting for transfers between devices  60.5 us (13%)
  starting transfers between devices  43.2 us (9%)
  local copies, waits for them, and re-layouts  34.4 us (8%)
  other arithmetic  17.3 us (4%)
  between operations  14.9 us (3%)
    all_gather x1, blocking collectives, per_device(): raw_all = lax.all_gather(raw, ('dp', 'tensor'), axis=0, tiled=False)  149 us
    ppermute x3, waiting for transfers between devices, summed_slab(): lax.ppermute(row_top, 'tensor', perm)  38 us
    dot_general x3, matrix products, summed_slab(): part = jnp.dot(hidden, block, preferred_element_type=jnp.float32)  29.4 us
    all_gather x1, blocking collectives, per_device(): lax.all_gather(jnp.stack((inverse, pull)), 'dp', axis=0, tiled=False)  26.7 us
    ppermute x3, starting transfers between devices, summed_slab(): lax.ppermute(row_top, 'tensor', perm)  25.4 us
    dot_general x1, matrix products, per_device(): lax.dot_general(hidden_all, d_cols.reshape(shards * tok_rows, col_width),...  24.1 us
    dot_general x1, matrix products, per_device(): lax.dot_general(d_low, down_weight, (((1,), (1,)), ((), ())), preferred_e...  23.3 us
    ppermute x7, waiting for transfers between devices, exchanged_tokens(): block = lax.ppermute(block, 'dp', flip_perm(count, mask))  21.8 us
  transfers between devices with their start and end apart: 17, of which 4 were waited for; matrix products, arithmetic and copies ran while one was open for 24% of the time, Pallas kernels for 0%

profile of v2, /device:TPU:0, one launch (start us, length us, event | category | flops | bytes accessed | tf_op | source)
XLA Modules:
  0.0 447.3 jit_solution(2600635963121039720)
XLA Ops:
  7.2 0.7 all-gather.6.cloned.1.call-update
  7.9 9.5 %abs_reduce_fusion = (f32[512]{0:T(512)S(1)}, f32[1024,512]{1,0:T(8,128)}) fusion(bf16[512,3584]{1,0:T(8,128)(2,1)} %param.6, bf16[3584,4096]{1,0:T(8,128)(2,1)} %param.7, s32[]{:T(128)S(6)} %select_n.81), kind=kOutput, calls=%fused_computation.38 | convolution fusion | flops 3759144448 | bytes 13109252 | tf_op jit(solution)/shard_map/dot_general | solution.py:35
  17.4 1.9 copy.31
  19.3 0.3 fusion.26
  19.7 5.5 %collective-permute-start.4 = (f16[512,1024]{1,0:T(8,128)(2,1)S(1)}, f16[512,1024]{1,0:T(8,128)(2,1)}, u32[]{:S(2)}, u32[]{:S(2)}) collective-permute-start(f16[512,1024]{1,0:T(8,128)(2,1)S(1)} %fusion.26), channel_id=1, source_target_pairs={{0,3},{1,0},{2,1},{3,2},{4,7},{5,4},{6,5},{7,6},{8,11},{9,8},{10,9... | collective-permute-start | bytes 3145736 | tf_op jit(solution)/shard_map/ppermute | solution.py:39
  25.2 10.4 %abs_reduce_fusion.1 = (f32[512]{0:T(512)S(1)}, f32[1024,512]{1,0:T(8,128)}) fusion(bf16[512,3584]{1,0:T(8,128)(2,1)} %param.6, bf16[3584,4096]{1,0:T(8,128)(2,1)} %param.7, s32[]{:T(128)S(6)} %select_n.80), kind=kOutput, calls=%fused_computation.40 | convolution fusion | flops 3759144448 | bytes 13109252 | tf_op jit(solution)/shard_map/dot_general | solution.py:35
  35.6 1.9 copy.30
  37.6 1.3 fusion.25
  39.1 9.5 %abs_reduce_fusion.2 = (f32[512]{0:T(512)S(1)}, f32[1024,512]{1,0:T(8,128)}) fusion(bf16[512,3584]{1,0:T(8,128)(2,1)} %param.6, bf16[3584,4096]{1,0:T(8,128)(2,1)} %param.7, s32[]{:T(128)S(6)} %select_n.79), kind=kOutput, calls=%fused_computation.42 | convolution fusion | flops 3759144448 | bytes 13109252 | tf_op jit(solution)/shard_map/dot_general | solution.py:35
  48.5 1.9 copy.29
  50.5 1.3 fusion.24
  51.8 1.8 collective-permute-start
  53.6 2.0 collective-permute-start.5
  55.6 0.6 collective-permute-start.3
  56.2 36.6 %collective-permute-done.5 = f32[512,1]{0,1:T(1,128)S(1)} collective-permute-done((f32[512,1]{0,1:T(1,128)S(1)}, f32[512,1]{0,1:T(1,128)S(1)}, u32[]{:S(2)}, u32[]{:S(2)}) %collective-permute-start.5) | collective-permute-done | bytes 2080 | tf_op jit(solution)/shard_map/ppermute | solution.py:39
  92.8 22.8 %collective-permute-start.1 = (f32[512,1]{0,1:T(1,128)S(1)}, f32[512,1]{0,1:T(1,128)S(1)}, u32[]{:S(2)}, u32[]{:S(2)}) collective-permute-start(f32[512,1]{0,1:T(1,128)S(1)} %bitcast.122), channel_id=1, source_target_pairs={{0,2},{1,3},{2,0},{3,1},{4,6},{5,7},{6,4},{7,5},{8,10},{9,11},{10,... | collective-permute-start | bytes 6152 | tf_op jit(solution)/shard_map/ppermute | solution.py:39
  115.8 1.4 collective-permute-done.1
  117.2 1.0 copy-done.3
  118.2 10.8 %fusion.47 = (bf16[512,1024]{1,0:T(8,128)(2,1)}, f32[512]{0:T(512)S(1)}, f32[512,1024]{1,0:T(8,128)S(1)}) fusion(f32[512]{0:T(512)S(1)} %bitcast.124, f16[512,1024]{1,0:T(8,128)(2,1)} %collective-permute-done.4, f32[512]{0:T(512)S(1)} %bitcast.125, f16[512,1024]{1,0:T(8,128)(2,1)} %collective-permute-done.2, f32[512]{0:T(512)S(1)} %bitcast.126, ...), kind=kOutput, calls=%fused_computation.111 | convolution fusion | flops 3765435904 | bytes 18358276 | tf_op jit(solution)/shard_map/dot_general | solution.py:41
  128.9 12.3 %psum.7 = f32[512]{0:T(512)S(1)} all-reduce(f32[512]{0:T(512)S(1)} %get-tuple-element.36), channel_id=1, replica_groups=mesh['dp'=8,'tensor'=4] {'tensor'}, use_global_device_ids=true, to_apply=%region_4.0 | all-reduce | flops 512 | bytes 4096 | tf_op jit(solution)/shard_map/psum | solution.py:111
  141.3 0.3 collective-permute-start.7
  141.6 3.5 collective-permute-start.8
  145.2 0.2 bitcast_reduce_fusion
  145.4 148.9 %all-gather.2 = f32[32,4,1024]{2,1,0:T(4,128)S(1)} all-gather(f32[1,4,1024]{2,1,0:T(4,128)S(1)} %multiply_bitcast_fusion), channel_id=2, replica_groups=mesh['dp'=8,'tensor'=4] {'dp','tensor'}, dimensions={0}, use_global_device_ids=true | all-gather | bytes 540672 | tf_op jit(solution)/shard_map/all_gather | solution.py:117
  294.3 1.1 copy.32
  295.4 1.6 reshape.143
  297.0 0.3 copy_multiply_fusion.1
  297.3 0.2 fusion.31
  297.5 0.6 fusion.38
  298.1 0.2 multiply_reduce_fusion.2
  298.3 0.5 fusion.18
  298.8 0.4 fusion.15
  299.3 0.4 copy.34
  299.7 1.2 reshape.144
  300.8 1.9 broadcast_multiply_fusion.1
  302.7 1.3 stack.26
  304.1 1.7 fusion.27
  305.7 0.6 dynamic_slice.63
  306.3 1.0 dynamic_slice.53
  307.3 0.8 constant_dynamic-slice_fusion.7
  308.2 0.5 broadcast_in_dim.28
  308.7 1.3 constant_dynamic-update-slice_fusion.3
  310.0 0.9 constant_dynamic-slice_fusion.8
  310.9 1.3 constant_dynamic-update-slice_fusion.2
  312.3 1.3 constant_dynamic-update-slice_fusion.1
  313.7 1.3 constant_dynamic-update-slice_fusion
  315.0 0.9 fusion.2
  316.0 4.3 fusion.1
  320.3 1.5 constant_dynamic-slice_fusion
  321.8 23.3 %convolution_convert_fusion = bf16[512,3584]{1,0:T(8,128)(2,1)} fusion(bf16[512,4096]{1,0:T(8,128)(2,1)} %fusion.1, bf16[3584,4096]{1,0:T(8,128)(2,1)} %param.7), kind=kOutput, calls=%fused_computation.19 | convolution fusion | flops 15034220544 | bytes 37224448 | tf_op jit(solution)/shard_map/dot_general | solution.py:134
  345.0 1.3 fusion.20
  346.3 1.9 collective-permute-start.11
  348.2 1.4 collective-permute-start.12
  349.6 0.2 collective-permute-start.13
  349.8 26.7 %all-gather.3 = f32[8,2,512]{2,1,0:T(2,128)S(1)} all-gather(f32[1,2,512]{2,1,0:T(2,128)S(1)} %maximum_bitcast_fusion), channel_id=3, replica_groups=mesh['dp'=8,'tensor'=4] {'dp'}, dimensions={0}, use_global_device_ids=true | all-gather | bytes 36864 | tf_op jit(solution)/shard_map/all_gather | solution.py:143
  376.6 0.4 broadcast_in_dim.29
  377.0 1.1 bitcast_dynamic-update-slice_fusion.7
  378.1 2.9 collective-permute-start.14
  380.9 1.1 bitcast_dynamic-update-slice_fusion.6
  382.3 11.4 %collective-permute-done.14 = bf16[512,512]{1,0:T(8,128)(2,1)S(1)} collective-permute-done((bf16[512,512]{1,0:T(8,128)(2,1)S(1)}, bf16[512,512]{1,0:T(8,128)(2,1)S(1)}, u32[]{:S(2)}, u32[]{:S(2)}) %collective-permute-start.14) | collective-permute-done | bytes 524320 | tf_op jit(solution)/shard_map/ppermute | solution.py:67
  393.8 10.3 %collective-permute-done.15 = bf16[512,512]{1,0:T(8,128)(2,1)S(1)} collective-permute-done((bf16[512,512]{1,0:T(8,128)(2,1)S(1)}, bf16[512,512]{1,0:T(8,128)(2,1)S(1)}, u32[]{:S(2)}, u32[]{:S(2)}) %collective-permute-start.15) | collective-permute-done | bytes 524320 | tf_op jit(solution)/shard_map/ppermute | solution.py:67
  404.2 3.3 fusion.4
  407.5 24.1 %convolution_bitcast_fusion = f32[3584,512]{0,1:T(8,128)} fusion(bf16[4096,512]{1,0:T(8,128)(2,1)} %fusion.4, bf16[4096,3584]{1,0:T(8,128)(2,1)} %all-gather.6.cloned.1.call-done), kind=kOutput, calls=%fused_computation.18 | convolution fusion | flops 15032385536 | bytes 40894464 | tf_op jit(solution)/shard_map/dot_general | solution.py:149
  431.6 8.4 %copy.37 = f32[3584,512]{1,0:T(8,128)} copy(f32[3584,512]{0,1:T(8,128)} %convolution_bitcast_fusion) | data formatting | bytes 14680064
  (46 shorter events, 0.9 us)
Async XLA Ops:
  7.2 400.3 %all-gather.6.cloned.1.call-start = ((), (), s32[]{:S(2)}) async-start(), calls=%async_computation | async-start | bytes 33030144 | tf_op jit(solution)/shard_map/all_gather | solution.py:109
  19.7 97.5 %collective-permute-start.4 = (f16[512,1024]{1,0:T(8,128)(2,1)S(1)}, f16[512,1024]{1,0:T(8,128)(2,1)}, u32[]{:S(2)}, u32[]{:S(2)}) collective-permute-start(f16[512,1024]{1,0:T(8,128)(2,1)S(1)} %fusion.26), channel_id=1, source_target_pairs={{0,3},{1,0},{2,1},{3,2},{4,7},{5,4},{6,5},{7,6},{8,11},{9,8},{10,9... | collective-permute-start | bytes 3145736 | tf_op jit(solution)/shard_map/ppermute | solution.py:39
  38.9 78.3 %collective-permute-start.2 = (f16[512,1024]{1,0:T(8,128)(2,1)}, f16[512,1024]{1,0:T(8,128)(2,1)}, u32[]{:S(2)}, u32[]{:S(2)}) collective-permute-start(f16[512,1024]{1,0:T(8,128)(2,1)} %fusion.25), channel_id=1, source_target_pairs={{0,1},{1,2},{2,3},{3,0},{4,5},{5,6},{6,7},{7,4},{8,9},{9,10},{10,1... | collective-permute-start | bytes 3145736 | tf_op jit(solution)/shard_map/ppermute | solution.py:39
  48.5 7.7 %copy-start.1 = (f32[4096]{0:T(1024)S(1)}, f32[4096]{0:T(1024)}, u32[]{:S(2)}) copy-start(f32[4096]{0:T(1024)} %param.8) | copy-start | bytes 49156
  48.5 67.1 %copy-start.2 = (s32[8]{0:T(128)S(1)}, s32[8]{0:T(128)}, u32[]{:S(2)}) copy-start(s32[8]{0:T(128)} %param.9) | copy-start | bytes 100
  51.8 65.4 %collective-permute-start = (f16[512,1024]{1,0:T(8,128)(2,1)}, f16[512,1024]{1,0:T(8,128)(2,1)S(1)}, u32[]{:S(2)}, u32[]{:S(2)}) collective-permute-start(f16[512,1024]{1,0:T(8,128)(2,1)} %fusion.24), channel_id=1, source_target_pairs={{0,2},{1,3},{2,0},{3,1},{4,6},{5,7},{6,4},{7,5},{8,10},{9,11},{10,... | collective-permute-start | bytes 3145736 | tf_op jit(solution)/shard_map/ppermute | solution.py:39
  53.6 39.2 %collective-permute-start.5 = (f32[512,1]{0,1:T(1,128)S(1)}, f32[512,1]{0,1:T(1,128)S(1)}, u32[]{:S(2)}, u32[]{:S(2)}) collective-permute-start(f32[512,1]{0,1:T(1,128)S(1)} %bitcast.123), channel_id=1, source_target_pairs={{0,3},{1,0},{2,1},{3,2},{4,7},{5,4},{6,5},{7,6},{8,11},{9,8},{10,9... | collective-permute-start | bytes 6152 | tf_op jit(solution)/shard_map/ppermute | solution.py:39
  55.6 60.2 %collective-permute-start.3 = (f32[512,1]{0,1:T(1,128)S(1)}, f32[512,1]{0,1:T(1,128)S(1)}, u32[]{:S(2)}, u32[]{:S(2)}) collective-permute-start(f32[512,1]{0,1:T(1,128)S(1)} %bitcast.121), channel_id=1, source_target_pairs={{0,1},{1,2},{2,3},{3,0},{4,5},{5,6},{6,7},{7,4},{8,9},{9,10},{10,1... | collective-permute-start | bytes 6152 | tf_op jit(solution)/shard_map/ppermute | solution.py:39
  92.8 24.4 %collective-permute-start.1 = (f32[512,1]{0,1:T(1,128)S(1)}, f32[512,1]{0,1:T(1,128)S(1)}, u32[]{:S(2)}, u32[]{:S(2)}) collective-permute-start(f32[512,1]{0,1:T(1,128)S(1)} %bitcast.122), channel_id=1, source_target_pairs={{0,2},{1,3},{2,0},{3,1},{4,6},{5,7},{6,4},{7,5},{8,10},{9,11},{10,... | collective-permute-start | bytes 6152 | tf_op jit(solution)/shard_map/ppermute | solution.py:39
  117.2 1.0 copy-start.3
  141.3 169.6 %collective-permute-start.6 = (bf16[512,1024]{1,0:T(8,128)(2,1)}, bf16[512,1024]{1,0:T(8,128)(2,1)}, u32[]{:S(2)}, u32[]{:S(2)}) collective-permute-start(bf16[512,1024]{1,0:T(8,128)(2,1)} %get-tuple-element.7), channel_id=1, source_target_pairs={{0,1},{1,2},{2,3},{3,0},{4,5},{5,6},{6,7},{7,4},{8,9},{9,10},{10,1... | collective-permute-start | bytes 3145736 | tf_op jit(solution)/shard_map/ppermute | solution.py:52
  141.3 171.0 %collective-permute-start.7 = (bf16[512,1024]{1,0:T(8,128)(2,1)}, bf16[512,1024]{1,0:T(8,128)(2,1)}, u32[]{:S(2)}, u32[]{:S(2)}) collective-permute-start(bf16[512,1024]{1,0:T(8,128)(2,1)} %get-tuple-element.7), channel_id=1, source_target_pairs={{0,2},{1,3},{2,0},{3,1},{4,6},{5,7},{6,4},{7,5},{8,10},{9,11},{10,... | collective-permute-start | bytes 3145736 | tf_op jit(solution)/shard_map/ppermute | solution.py:52
  141.6 172.1 %collective-permute-start.8 = (bf16[512,1024]{1,0:T(8,128)(2,1)}, bf16[512,1024]{1,0:T(8,128)(2,1)}, u32[]{:S(2)}, u32[]{:S(2)}) collective-permute-start(bf16[512,1024]{1,0:T(8,128)(2,1)} %get-tuple-element.7), channel_id=1, source_target_pairs={{0,3},{1,0},{2,1},{3,2},{4,7},{5,4},{6,5},{7,6},{8,11},{9,8},{10,9... | collective-permute-start | bytes 3145736 | tf_op jit(solution)/shard_map/ppermute | solution.py:52
  315.0 5.2 %copy-start = (bf16[512,4096]{1,0:T(8,128)(2,1)}, bf16[512,4096]{1,0:T(8,128)(2,1)S(1)}, u32[]{:S(2)}) copy-start(bf16[512,4096]{1,0:T(8,128)(2,1)S(1)} %constant_dynamic-update-slice_fusion) | copy-start | bytes 12582916
  321.8 56.3 %collective-permute-start.9 = (bf16[512,512]{1,0:T(8,128)(2,1)}, bf16[512,512]{1,0:T(8,128)(2,1)}, u32[]{:S(2)}, u32[]{:S(2)}) collective-permute-start(bf16[512,512]{1,0:T(8,128)(2,1)} %get-tuple-element.34), channel_id=1, source_target_pairs={{0,4},{4,0},{8,12},{12,8},{16,20},{20,16},{24,28},{28,24},{1,5},{5... | collective-permute-start | bytes 1572872 | tf_op jit(solution)/shard_map/ppermute | solution.py:67
  346.3 35.7 %collective-permute-start.10 = (bf16[512,512]{1,0:T(8,128)(2,1)}, bf16[512,512]{1,0:T(8,128)(2,1)S(1)}, u32[]{:S(2)}, u32[]{:S(2)}) collective-permute-start(bf16[512,512]{1,0:T(8,128)(2,1)} %get-tuple-element.33), channel_id=1, source_target_pairs={{0,8},{4,12},{8,0},{12,4},{16,24},{20,28},{24,16},{28,20},{1,9},{5... | collective-permute-start | bytes 1572872 | tf_op jit(solution)/shard_map/ppermute | solution.py:67
  346.3 35.8 %collective-permute-start.11 = (bf16[512,512]{1,0:T(8,128)(2,1)}, bf16[512,512]{1,0:T(8,128)(2,1)S(1)}, u32[]{:S(2)}, u32[]{:S(2)}) collective-permute-start(bf16[512,512]{1,0:T(8,128)(2,1)} %get-tuple-element.32), channel_id=1, source_target_pairs={{0,12},{4,8},{8,4},{12,0},{16,28},{20,24},{24,20},{28,16},{1,13},{... | collective-permute-start | bytes 1572872 | tf_op jit(solution)/shard_map/ppermute | solution.py:67
  348.2 34.0 %collective-permute-start.12 = (bf16[512,512]{1,0:T(8,128)(2,1)}, bf16[512,512]{1,0:T(8,128)(2,1)S(1)}, u32[]{:S(2)}, u32[]{:S(2)}) collective-permute-start(bf16[512,512]{1,0:T(8,128)(2,1)} %get-tuple-element.31), channel_id=1, source_target_pairs={{0,16},{4,20},{8,24},{12,28},{16,0},{20,4},{24,8},{28,12},{1,17},{... | collective-permute-start | bytes 1572872 | tf_op jit(solution)/shard_map/ppermute | solution.py:67
  349.6 32.6 %collective-permute-start.13 = (bf16[512,512]{1,0:T(8,128)(2,1)}, bf16[512,512]{1,0:T(8,128)(2,1)S(1)}, u32[]{:S(2)}, u32[]{:S(2)}) collective-permute-start(bf16[512,512]{1,0:T(8,128)(2,1)} %get-tuple-element.30), channel_id=1, source_target_pairs={{0,20},{4,16},{8,28},{12,24},{16,4},{20,0},{24,12},{28,8},{1,21},{... | collective-permute-start | bytes 1572872 | tf_op jit(solution)/shard_map/ppermute | solution.py:67
  378.1 15.7 %collective-permute-start.14 = (bf16[512,512]{1,0:T(8,128)(2,1)S(1)}, bf16[512,512]{1,0:T(8,128)(2,1)S(1)}, u32[]{:S(2)}, u32[]{:S(2)}) collective-permute-start(bf16[512,512]{1,0:T(8,128)(2,1)S(1)} %get-tuple-element.29), channel_id=1, source_target_pairs={{0,24},{4,28},{8,16},{12,20},{16,8},{20,12},{24,0},{28,4},{1,25},{... | collective-permute-start | bytes 1572872 | tf_op jit(solution)/shard_map/ppermute | solution.py:67
  382.0 22.1 %collective-permute-start.15 = (bf16[512,512]{1,0:T(8,128)(2,1)S(1)}, bf16[512,512]{1,0:T(8,128)(2,1)S(1)}, u32[]{:S(2)}, u32[]{:S(2)}) collective-permute-start(bf16[512,512]{1,0:T(8,128)(2,1)S(1)} %get-tuple-element.28), channel_id=1, source_target_pairs={{0,28},{4,24},{8,20},{12,16},{16,12},{20,8},{24,4},{28,0},{1,29},{... | collective-permute-start | bytes 1572872 | tf_op jit(solution)/shard_map/ppermute | solution.py:67
Sparse Core Ops, SparseCore 0:
  9.9 145.7 all-gather.5
